TPU v7x, 32 devices: a whole 2x2x4 slice. The times are simulated.
32 devices in a mesh: row: 8 (over y, x, core), col: 4 (over z).
Axes of the slice: x: 2, y: 2, z: 4, core: 2. Of those that a mesh axis runs over, the one named last changes fastest.
Arguments:
- tokens: bfloat16 [448, 8192], P('col', 'row'), may hold values from -6 to 6
- gate_weight: bfloat16 [8192, 26624], P('row', 'col'), may hold values from -0.0625 to 0.0625
- up_weight: bfloat16 [8192, 26624], P('row', 'col'), may hold values from -0.0625 to 0.0625
- down_weight: bfloat16 [26624, 8192], P('col', 'row'), may hold values from -0.0390625 to 0.0390625
- cotangent: bfloat16 [448, 8192], P('col', 'row'), may hold values from -6 to 6
Outputs:
- layer_out: bfloat16 [448, 8192], P('col', 'row')
- token_grad: bfloat16 [448, 8192], P('col', 'row')
- gate_grad: bfloat16 [8192, 26624], P('row', 'col')
- up_grad: bfloat16 [8192, 26624], P('row', 'col')
- down_grad: bfloat16 [26624, 8192], P('col', 'row')
All inputs are finite; a program needn't handle non-finite values.
Results may differ from a plain program's by a relative error of at most 0.0051.
Values may be sent and summed in bfloat16 or wider, within the bound.
A program may use at most 256 MiB of HBM per device.

v0:
```python
import jax
import jax.numpy as jnp
from jax import lax
from jax.sharding import PartitionSpec as P

F32, BF16 = jnp.float32, jnp.bfloat16


def contract(left, right, left_dim, right_dim):
    return lax.dot_general(
        left, right, (((left_dim,), (right_dim,)), ((), ())), preferred_element_type=F32
    )


def swap(value, size, bit):
    return lax.ppermute(value, "row", [(i, i ^ bit) for i in range(size)])


def after(value, *earlier):
    for other in earlier:
        first = lax.slice(other, (0,) * other.ndim, (1,) * other.ndim).reshape(())
        value = value + (first.astype(F32) * 0.0).astype(value.dtype)
    return value


def scatter_col(share, size):
    me = lax.axis_index("col")
    rows = share.shape[0] // size
    part = lambda k: lax.dynamic_slice(share, (k % size * rows, 0), (rows, share.shape[1]))
    sent = [
        lax.ppermute(part(me + s).astype(BF16), "col", [(i, (i + s) % size) for i in range(size)])
        for s in range(1, size)
    ]
    total = part(me)
    for got in sent:
        total = total + got.astype(F32)
    return total.astype(BF16)


def gather_col(block, size):
    me = lax.axis_index("col")
    rows = block.shape[0]
    out = jnp.zeros((size * rows, block.shape[1]), block.dtype)
    out = lax.dynamic_update_slice(out, block, (me * rows, 0))
    for shift in range(1, size):
        got = lax.ppermute(block, "col", [(i, (i + shift) % size) for i in range(size)])
        out = lax.dynamic_update_slice(out, got, (((me - shift + size) % size) * rows, 0))
    return out


def reorder(value, size, me):
    blocks = value.reshape(size, -1, value.shape[1])
    index = jnp.arange(size) ^ me
    return jnp.take(blocks, index, axis=0, mode="clip").reshape(value.shape)


def make_body(rows, cols):
    bits = rows.bit_length() - 1
    link_bits = list(range(1, bits))

    def body(tokens, gate_weight, up_weight, down_weight, cotangent):
        me = lax.axis_index("row")
        col_tokens = gather_col(tokens, cols)
        all_tokens = reorder(col_tokens, rows, me)
        all_cotangent = reorder(gather_col(after(cotangent, col_tokens), cols), rows, me)
        units = gate_weight.shape[1]
        half = units // 2
        spans = ((0, half), (half, units))
        count = all_tokens.shape[0]
        small = count // rows

        def split_core(value):
            v = value.reshape(rows // 2, 2, small, value.shape[1])
            return [v[:, i].reshape(count // 2, value.shape[1]) for i in range(2)]

        tok_keep, tok_send = split_core(all_tokens)
        cot_keep, cot_send = split_core(all_cotangent)
        tok_all = jnp.concatenate([tok_keep, tok_send], 0)
        cot_all = jnp.concatenate([cot_keep, cot_send], 0)

        def scatter(total, which):
            width = total.shape[1]
            shape = [2] * (bits - 1)
            total = total.reshape(shape + [small, width])
            live = list(reversed(link_bits))
            order = list(live) if which == 0 else list(reversed(live))
            for bit in order:
                axis = live.index(bit)
                send = lax.index_in_dim(total, 1, axis, keepdims=False).astype(BF16)
                keep = lax.index_in_dim(total, 0, axis, keepdims=False)
                total = keep + swap(send, rows, 1 << bit).astype(F32)
                live.remove(bit)
            return total

        def gather(block, which, before_core):
            total = block
            full = list(reversed(link_bits))
            order = full if which == 0 else list(reversed(full))
            live = []
            for bit in reversed(order):
                got = swap(total, rows, 1 << bit)
                live = sorted(live + [bit], reverse=True)
                total = jnp.stack([total, got], axis=live.index(bit))
            total = after(total.reshape(count // 2, block.shape[1]), *before_core)
            return jnp.concatenate([total, swap(total, rows, 1)], 0), total

        def shares(left, weight, transposed):
            out = []
            for a, b in spans:
                if transposed:
                    out.append(contract(left, weight[a:b], 1, 1))
                else:
                    out.append(contract(left, weight[:, a:b], 1, 0))
            return out

        def cores(sends):
            return [swap(x, rows, 1) for x in sends]

        def sums(keeps, gots):
            return [scatter(k + g, i) for i, (k, g) in enumerate(zip(keeps, gots))]

        gate_send = shares(tok_send, gate_weight, False)
        gate_got = cores(gate_send)
        up_send = shares(after(tok_send, gate_send[1]), up_weight, False)
        up_got = cores(up_send)
        gate_keep = shares(after(tok_keep, up_send[1]), gate_weight, False)
        gate = sums(gate_keep, gate_got)
        hid_send = shares(after(cot_send, gate_keep[1]), down_weight, True)
        hid_got = cores(hid_send)
        up_keep = shares(after(tok_keep, hid_send[1]), up_weight, False)
        up = sums(up_keep, up_got)
        hidden, gate_delta, up_delta = [], [], []
        activated, slope = [], []
        for i in range(2):
            sigmoid_gate = jax.nn.sigmoid(gate[i])
            activated.append(gate[i] * sigmoid_gate)
            hidden.append((activated[i] * up[i]).astype(BF16))
            slope.append(up[i] * sigmoid_gate * (1.0 + gate[i] * (1.0 - sigmoid_gate)))
        hid_keep = shares(after(cot_keep, *hidden), down_weight, True)
        hid = sums(hid_keep, hid_got)
        for i in range(2):
            up_delta.append((hid[i] * activated[i]).astype(BF16))
            gate_delta.append((hid[i] * slope[i]).astype(BF16))

        def join(blocks, links_free, before_core, *earlier):
            both = [gather(after(b, *links_free), i, before_core) for i, b in enumerate(blocks)]
            return jnp.concatenate([after(x, *earlier) for x, _ in both], 1), [t for _, t in both]

        hiddens, _ = join(hidden, [], [], *hid_keep)
        tokens_t = lax.optimization_barrier(tok_all.T)
        out_share = jnp.dot(hiddens, down_weight, preferred_element_type=F32)
        down_grad = contract(hiddens, after(cot_all, out_share), 0, 0).astype(BF16)
        gate_deltas, gate_mid = join(gate_delta, [], [], down_grad)
        gate_grad = jnp.dot(tokens_t, gate_deltas, preferred_element_type=F32).astype(BF16)
        token_share = contract(after(gate_deltas, gate_grad), gate_weight, 1, 1)
        up_deltas, _ = join(up_delta, gate_mid, [gate_grad], token_share)
        token_share = token_share + contract(up_deltas, up_weight, 1, 1)
        up_grad = jnp.dot(
            after(tokens_t, token_share), up_deltas, preferred_element_type=F32
        ).astype(BF16)

        def to_global(value):
            keep, send = value[: count // 2], value[count // 2 :]
            both = jnp.stack(
                [x.reshape(rows // 2, small, x.shape[1]) for x in (keep, send)], 1
            ).reshape(value.shape)
            return reorder(both, rows, me)

        layer_out = scatter_col(to_global(out_share), cols)
        token_grad = scatter_col(to_global(token_share), cols)
        return (layer_out, token_grad, gate_grad, up_grad, down_grad)

    return body


def solution(mesh):
    placed = (P("col", "row"), P("row", "col"), P("row", "col"), P("col", "row"), P("col", "row"))
    return jax.shard_map(
        make_body(mesh.shape["row"], mesh.shape["col"]),
        mesh=mesh,
        in_specs=placed,
        out_specs=(
            P("col", "row"),
            P("col", "row"),
            P("row", "col"),
            P("row", "col"),
            P("col", "row"),
        ),
        check_vma=False,
    )
```

profile of v0, /device:TPU:0, one launch (start us, length us, event | category | flops | bytes accessed | tf_op | source)
XLA Modules:
  0.0 375.0 jit_solution(17190190656457643357)
XLA Ops:
  7.8 4.6 %collective-permute-done = bf16[112,1024]{1,0:T(8,128)(2,1)S(1)} collective-permute-done((bf16[112,1024]{1,0:T(8,128)(2,1)}, bf16[112,1024]{1,0:T(8,128)(2,1)S(1)}, u32[]{:S(2)}, u32[]{:S(2)}) %collective-permute-start) | collective-permute-done | bytes 229408 | tf_op jit(solution)/shard_map/ppermute | solution.py:46
  12.4 13.8 %collective-permute-done.1 = bf16[112,1024]{1,0:T(8,128)(2,1)S(1)} collective-permute-done((bf16[112,1024]{1,0:T(8,128)(2,1)}, bf16[112,1024]{1,0:T(8,128)(2,1)S(1)}, u32[]{:S(2)}, u32[]{:S(2)}) %collective-permute-start.1) | collective-permute-done | bytes 229408 | tf_op jit(solution)/shard_map/ppermute | solution.py:46
  27.1 6.8 %fusion.12 = f32[224,3328]{1,0:T(8,128)} fusion(bf16[224,1024]{1,0:T(8,128)(2,1)S(1)} %bitcast.236, bf16[1024,6656]{1,0:T(8,128)(2,1)} %param.6), kind=kOutput, calls=%fused_computation.19 | convolution fusion | flops 1526726656 | bytes 10256384 | tf_op jit(solution)/shard_map/dot_general | solution.py:10
  33.9 6.4 %fusion.22 = f32[224,3328]{1,0:T(8,128)} fusion(bf16[224,1024]{1,0:T(8,128)(2,1)S(1)} %bitcast.237, bf16[1024,6656]{1,0:T(8,128)(2,1)} %param.6), kind=kOutput, calls=%fused_computation.29 | convolution fusion | flops 1526726656 | bytes 10256384 | tf_op jit(solution)/shard_map/dot_general | solution.py:10
  62.0 5.7 %fusion.29 = f32[224,3328]{1,0:T(8,128)S(1)} fusion(f32[224,3328]{1,0:T(8,128)} %collective-permute-done.3, bf16[1024,6656]{1,0:T(8,128)(2,1)} %param.6, bf16[224,1024]{1,0:T(8,128)(2,1)S(1)} %bitcast.223, bf16[]{:T(256)} %bitcast.6), kind=kOutput, calls=%fused_computation.37 | convolution fusion | flops 1527701504 | bytes 13238784 | tf_op jit(solution)/shard_map/dot_general | solution.py:10
  67.8 7.3 %fusion.106 = (f32[224,3328]{1,0:T(8,128)S(1)}, f32[224,3328]{1,0:T(8,128)S(1)}) fusion(f32[224,3328]{1,0:T(8,128)} %collective-permute-done.15, bf16[1024,6656]{1,0:T(8,128)(2,1)} %param.6, bf16[224,1024]{1,0:T(8,128)(2,1)S(1)} %bitcast.224, bf16[]{:T(256)} %bitcast.6), kind=kOutput, calls=%fused_computation.184 | convolution fusion | flops 1527701504 | bytes 16220672 | tf_op jit(solution)/shard_map/dot_general | solution.py:10
  85.2 5.5 %fusion.26 = f32[224,3328]{1,0:T(8,128)S(1)} fusion(f32[224,3328]{1,0:T(8,128)} %collective-permute-done.18, bf16[1024,6656]{1,0:T(8,128)(2,1)} %param.7, bf16[224,1024]{1,0:T(8,128)(2,1)S(1)} %bitcast.225, bf16[]{:T(256)} %bitcast.16), kind=kOutput, calls=%fused_computation.36 | convolution fusion | flops 1527701504 | bytes 13238784 | tf_op jit(solution)/shard_map/dot_general | solution.py:10
  90.8 5.5 %fusion.32 = f32[224,3328]{1,0:T(8,128)S(1)} fusion(f32[224,3328]{1,0:T(8,128)} %collective-permute-done.9, bf16[1024,6656]{1,0:T(8,128)(2,1)} %param.7, bf16[224,1024]{1,0:T(8,128)(2,1)S(1)} %bitcast.226, bf16[]{:T(256)} %bitcast.16), kind=kOutput, calls=%fused_computation.38 | convolution fusion | flops 1527701504 | bytes 13238784 | tf_op jit(solution)/shard_map/dot_general | solution.py:10
  104.3 14.3 %collective-permute-done.19 = bf16[2,56,3328]{2,1,0:T(8,128)(2,1)S(1)} collective-permute-done((bf16[2,56,3328]{2,1,0:T(8,128)(2,1)S(1)}, bf16[2,56,3328]{2,1,0:T(8,128)(2,1)S(1)}, u32[]{:S(2)}, u32[]{:S(2)}) %collective-permute-start.19) | collective-permute-done | bytes 745504 | tf_op jit(solution)/shard_map/ppermute | solution.py:16
  121.1 9.1 %collective-permute-done.17 = bf16[56,3328]{1,0:T(8,128)(2,1)S(1)} collective-permute-done((bf16[56,3328]{1,0:T(8,128)(2,1)S(1)}, bf16[56,3328]{1,0:T(8,128)(2,1)S(1)}, u32[]{:S(2)}, u32[]{:S(2)}) %collective-permute-start.17) | collective-permute-done | bytes 372768 | tf_op jit(solution)/shard_map/ppermute | solution.py:16
  140.0 4.5 %collective-permute-done.21 = bf16[56,3328]{1,0:T(8,128)(2,1)S(1)} collective-permute-done((bf16[56,3328]{1,0:T(8,128)(2,1)S(1)}, bf16[56,3328]{1,0:T(8,128)(2,1)S(1)}, u32[]{:S(2)}, u32[]{:S(2)}) %collective-permute-start.21) | collective-permute-done | bytes 372768 | tf_op jit(solution)/shard_map/ppermute | solution.py:16
  154.9 7.3 %collective-permute-done.22 = bf16[2,56,3328]{2,1,0:T(8,128)(2,1)} collective-permute-done((bf16[2,56,3328]{2,1,0:T(8,128)(2,1)}, bf16[2,56,3328]{2,1,0:T(8,128)(2,1)}, u32[]{:S(2)}, u32[]{:S(2)}) %collective-permute-start.22) | collective-permute-done | bytes 745504 | tf_op jit(solution)/shard_map/ppermute | solution.py:16
  167.1 7.8 %fusion.108 = (f32[224,3328]{1,0:T(8,128)S(1)}, f32[224,3328]{1,0:T(8,128)}) fusion(f32[224,3328]{1,0:T(8,128)} %collective-permute-done.27, bf16[6656,1024]{1,0:T(8,128)(2,1)} %param.8, bf16[224,1024]{1,0:T(8,128)(2,1)S(1)} %bitcast.216, bf16[]{:T(256)} %bitcast.38, bf16[]{:T(256)} %bitcast.27), kind=kOutput, calls=%fused_computation.186 | convolution fusion | flops 1527930880 | bytes 16221184 | tf_op jit(solution)/shard_map/dot_general | solution.py:10
  177.7 5.7 %fusion.107 = (f32[224,3328]{1,0:T(8,128)S(1)}, f32[224,3328]{1,0:T(8,128)}) fusion(f32[224,3328]{1,0:T(8,128)} %collective-permute-done.33, bf16[6656,1024]{1,0:T(8,128)(2,1)S(1)} %bitcast.194, bf16[224,1024]{1,0:T(8,128)(2,1)S(1)} %bitcast.217, bf16[]{:T(256)} %bitcast.38, bf16[]{:T(256)} %bitcast.27), kind=kOutput, calls=%fused_computation.185 | convolution fusion | flops 1527930880 | bytes 16220164 | tf_op jit(solution)/shard_map/dot_general | solution.py:10
  186.9 8.8 %collective-permute-done.28 = bf16[2,56,3328]{2,1,0:T(8,128)(2,1)S(1)} collective-permute-done((bf16[2,56,3328]{2,1,0:T(8,128)(2,1)S(1)}, bf16[2,56,3328]{2,1,0:T(8,128)(2,1)S(1)}, u32[]{:S(2)}, u32[]{:S(2)}) %collective-permute-start.28) | collective-permute-done | bytes 745504 | tf_op jit(solution)/shard_map/ppermute | solution.py:16
  198.2 6.8 %collective-permute-done.34 = bf16[2,56,3328]{2,1,0:T(8,128)(2,1)S(1)} collective-permute-done((bf16[2,56,3328]{2,1,0:T(8,128)(2,1)S(1)}, bf16[2,56,3328]{2,1,0:T(8,128)(2,1)S(1)}, u32[]{:S(2)}, u32[]{:S(2)}) %collective-permute-start.34) | collective-permute-done | bytes 745504 | tf_op jit(solution)/shard_map/ppermute | solution.py:16
  211.4 6.5 %fusion.36 = f32[448,1024]{1,0:T(8,128)S(1)} fusion(bf16[6656,1024]{1,0:T(8,128)(2,1)S(1)} %bitcast.194, bf16[448,3328]{1,0:T(8,128)(2,1)S(1)} %fusion.38, bf16[448,3328]{1,0:T(8,128)(2,1)S(1)} %fusion.37), kind=kOutput, calls=%fused_computation.40 | convolution fusion | flops 6118834176 | bytes 21430272 | tf_op jit(solution)/shard_map/dot_general | solution.py:151
  246.4 5.6 %collective-permute-done.36 = bf16[56,3328]{1,0:T(8,128)(2,1)S(1)} collective-permute-done((bf16[56,3328]{1,0:T(8,128)(2,1)S(1)}, bf16[56,3328]{1,0:T(8,128)(2,1)S(1)}, u32[]{:S(2)}, u32[]{:S(2)}) %collective-permute-start.36) | collective-permute-done | bytes 372768 | tf_op jit(solution)/shard_map/ppermute | solution.py:16
  253.0 11.6 %convolution_convert_fusion.2 = bf16[6656,1024]{1,0:T(8,128)(2,1)} fusion(bf16[448,3328]{1,0:T(8,128)(2,1)S(1)} %copy-done.15, bf16[448,3328]{1,0:T(8,128)(2,1)S(1)} %copy-done.17, bf16[224,1024]{1,0:T(8,128)(2,1)} %bitcast.255, bf16[224,1024]{1,0:T(8,128)(2,1)S(1)} %bitcast.218, bf16[]{:T(256)} %bitcast.61), kind=kOutput, calls=%fused_computation.6 | convolution fusion | flops 6128402432 | bytes 20512770 | tf_op jit(solution)/shard_map/dot_general | solution.py:10
  279.3 7.4 %collective-permute-done.39 = bf16[56,3328]{1,0:T(8,128)(2,1)S(1)} collective-permute-done((bf16[56,3328]{1,0:T(8,128)(2,1)S(1)}, bf16[56,3328]{1,0:T(8,128)(2,1)S(1)}, u32[]{:S(2)}, u32[]{:S(2)}) %collective-permute-start.39) | collective-permute-done | bytes 372768 | tf_op jit(solution)/shard_map/ppermute | solution.py:16
  292.6 10.5 %convolution_convert_fusion.1 = bf16[1024,6656]{1,0:T(8,128)(2,1)} fusion(bf16[1024,448]{0,1:T(8,128)(2,1)S(1)} %copy-done.27, bf16[448,3328]{1,0:T(8,128)(2,1)S(1)} %maximum_add_fusion.3, bf16[448,3328]{1,0:T(8,128)(2,1)S(1)} %maximum_add_fusion.2), kind=kOutput, calls=%fused_computation.5 | convolution fusion | flops 6125649920 | bytes 20512768 | tf_op jit(solution)/shard_map/dot_general | solution.py:154
  308.2 15.4 %fusion.24 = f32[448,1024]{1,0:T(8,128)} fusion(bf16[1024,6656]{1,0:T(8,128)(2,1)} %param.6, bf16[448,3328]{1,0:T(8,128)(2,1)} %copy-done.18, bf16[448,3328]{1,0:T(8,128)(2,1)} %copy-done.19, bf16[]{:T(256)} %bitcast.74), kind=kOutput, calls=%fused_computation.34 | convolution fusion | flops 6124797952 | bytes 21430274 | tf_op jit(solution)/shard_map/dot_general | solution.py:10
  332.4 14.2 %fusion.40 = f32[448,1024]{1,0:T(8,128)S(1)} fusion(f32[448,1024]{1,0:T(8,128)} %fusion.24, bf16[1024,6656]{1,0:T(8,128)(2,1)} %param.7, bf16[448,3328]{1,0:T(8,128)(2,1)} %maximum_add_fusion.5, bf16[448,3328]{1,0:T(8,128)(2,1)} %maximum_add_fusion.4), kind=kOutput, calls=%fused_computation.52 | convolution fusion | flops 6119292928 | bytes 23265280 | tf_op jit(solution)/shard_map/dot_general | solution.py:10
  355.3 13.2 %convolution_convert_fusion = bf16[1024,6656]{1,0:T(8,128)(2,1)} fusion(bf16[448,3328]{1,0:T(8,128)(2,1)} %maximum_add_fusion.5, bf16[448,3328]{1,0:T(8,128)(2,1)} %maximum_add_fusion.4, bf16[1024,448]{0,1:T(8,128)(2,1)S(1)} %copy-done.28, bf16[]{:T(256)} %bitcast.95), kind=kOutput, calls=%fused_computation.4 | convolution fusion | flops 6126108672 | bytes 20512770 | tf_op jit(solution)/shard_map/dot_general | solution.py:158
  (274 shorter events, 158.3 us)
Async XLA Ops:
  3.7 22.6 %collective-permute-start.2 = (bf16[112,1024]{1,0:T(8,128)(2,1)}, bf16[112,1024]{1,0:T(8,128)(2,1)S(1)}, u32[]{:S(2)}, u32[]{:S(2)}) collective-permute-start(bf16[112,1024]{1,0:T(8,128)(2,1)} %param.5), channel_id=1, source_target_pairs={{0,3},{1,0},{2,1},{3,2},{4,7},{5,4},{6,5},{7,6},{8,11},{9,8},{10,9... | collective-permute-start | bytes 688136 | tf_op jit(solution)/shard_map/ppermute | solution.py:46
  5.8 20.5 %collective-permute-start.1 = (bf16[112,1024]{1,0:T(8,128)(2,1)}, bf16[112,1024]{1,0:T(8,128)(2,1)S(1)}, u32[]{:S(2)}, u32[]{:S(2)}) collective-permute-start(bf16[112,1024]{1,0:T(8,128)(2,1)} %param.5), channel_id=1, source_target_pairs={{0,2},{1,3},{2,0},{3,1},{4,6},{5,7},{6,4},{7,5},{8,10},{9,11},{10,... | collective-permute-start | bytes 688136 | tf_op jit(solution)/shard_map/ppermute | solution.py:46
  33.9 28.1 %collective-permute-start.3 = (f32[224,3328]{1,0:T(8,128)}, f32[224,3328]{1,0:T(8,128)}, u32[]{:S(2)}, u32[]{:S(2)}) collective-permute-start(f32[224,3328]{1,0:T(8,128)} %fusion.12), channel_id=1, source_target_pairs={{0,4},{4,0},{8,12},{12,8},{16,20},{20,16},{24,28},{28,24},{1,5},{5... | collective-permute-start | bytes 8945672 | tf_op jit(solution)/shard_map/ppermute | solution.py:16
  40.3 27.5 %collective-permute-start.15 = (f32[224,3328]{1,0:T(8,128)}, f32[224,3328]{1,0:T(8,128)}, u32[]{:S(2)}, u32[]{:S(2)}) collective-permute-start(f32[224,3328]{1,0:T(8,128)} %fusion.22), channel_id=1, source_target_pairs={{0,4},{4,0},{8,12},{12,8},{16,20},{20,16},{24,28},{28,24},{1,5},{5... | collective-permute-start | bytes 8945672 | tf_op jit(solution)/shard_map/ppermute | solution.py:16
  56.6 28.7 %collective-permute-start.18 = (f32[224,3328]{1,0:T(8,128)}, f32[224,3328]{1,0:T(8,128)}, u32[]{:S(2)}, u32[]{:S(2)}) collective-permute-start(f32[224,3328]{1,0:T(8,128)} %fusion.18), channel_id=1, source_target_pairs={{0,4},{4,0},{8,12},{12,8},{16,20},{20,16},{24,28},{28,24},{1,5},{5... | collective-permute-start | bytes 8945672 | tf_op jit(solution)/shard_map/ppermute | solution.py:16
  59.5 31.3 %collective-permute-start.9 = (f32[224,3328]{1,0:T(8,128)}, f32[224,3328]{1,0:T(8,128)}, u32[]{:S(2)}, u32[]{:S(2)}) collective-permute-start(f32[224,3328]{1,0:T(8,128)} %fusion.4), channel_id=1, source_target_pairs={{0,4},{4,0},{8,12},{12,8},{16,20},{20,16},{24,28},{28,24},{1,5},{5... | collective-permute-start | bytes 8945672 | tf_op jit(solution)/shard_map/ppermute | solution.py:16
  81.4 96.2 %collective-permute-start.33 = (f32[224,3328]{1,0:T(8,128)}, f32[224,3328]{1,0:T(8,128)}, u32[]{:S(2)}, u32[]{:S(2)}) collective-permute-start(f32[224,3328]{1,0:T(8,128)} %fusion.10), channel_id=1, source_target_pairs={{0,4},{4,0},{8,12},{12,8},{16,20},{20,16},{24,28},{28,24},{1,5},{5... | collective-permute-start | bytes 8945672 | tf_op jit(solution)/shard_map/ppermute | solution.py:16
  81.4 20.6 %collective-permute-start.4 = (bf16[2,56,3328]{2,1,0:T(8,128)(2,1)S(1)}, bf16[2,56,3328]{2,1,0:T(8,128)(2,1)S(1)}, u32[]{:S(2)}, u32[]{:S(2)}) collective-permute-start(bf16[2,56,3328]{2,1,0:T(8,128)(2,1)S(1)} %bitcast.249), channel_id=1, source_target_pairs={{0,16},{4,20},{8,24},{12,28},{16,0},{20,4},{24,8},{28,12},{1,17},{... | collective-permute-start | bytes 2236424 | tf_op jit(solution)/shard_map/ppermute | solution.py:16
  83.0 19.6 %collective-permute-start.16 = (bf16[2,56,3328]{2,1,0:T(8,128)(2,1)S(1)}, bf16[2,56,3328]{2,1,0:T(8,128)(2,1)S(1)}, u32[]{:S(2)}, u32[]{:S(2)}) collective-permute-start(bf16[2,56,3328]{2,1,0:T(8,128)(2,1)S(1)} %fusion.47), channel_id=1, source_target_pairs={{0,8},{4,12},{8,0},{12,4},{16,24},{20,28},{24,16},{28,20},{1,9},{5... | collective-permute-start | bytes 2236424 | tf_op jit(solution)/shard_map/ppermute | solution.py:16
  96.5 22.8 %collective-permute-start.10 = (bf16[2,56,3328]{2,1,0:T(8,128)(2,1)S(1)}, bf16[2,56,3328]{2,1,0:T(8,128)(2,1)S(1)}, u32[]{:S(2)}, u32[]{:S(2)}) collective-permute-start(bf16[2,56,3328]{2,1,0:T(8,128)(2,1)S(1)} %bitcast.250), channel_id=1, source_target_pairs={{0,16},{4,20},{8,24},{12,28},{16,0},{20,4},{24,8},{28,12},{1,17},{... | collective-permute-start | bytes 2236424 | tf_op jit(solution)/shard_map/ppermute | solution.py:16
  97.1 21.5 %collective-permute-start.19 = (bf16[2,56,3328]{2,1,0:T(8,128)(2,1)S(1)}, bf16[2,56,3328]{2,1,0:T(8,128)(2,1)S(1)}, u32[]{:S(2)}, u32[]{:S(2)}) collective-permute-start(bf16[2,56,3328]{2,1,0:T(8,128)(2,1)S(1)} %fusion.48), channel_id=1, source_target_pairs={{0,8},{4,12},{8,0},{12,4},{16,24},{20,28},{24,16},{28,20},{1,9},{5... | collective-permute-start | bytes 2236424 | tf_op jit(solution)/shard_map/ppermute | solution.py:16
  102.0 65.1 %collective-permute-start.27 = (f32[224,3328]{1,0:T(8,128)}, f32[224,3328]{1,0:T(8,128)}, u32[]{:S(2)}, u32[]{:S(2)}) collective-permute-start(f32[224,3328]{1,0:T(8,128)} %fusion), channel_id=1, source_target_pairs={{0,4},{4,0},{8,12},{12,8},{16,20},{20,16},{24,28},{28,24},{1,5},{5... | collective-permute-start | bytes 8945672 | tf_op jit(solution)/shard_map/ppermute | solution.py:16
  102.6 34.1 %collective-permute-start.5 = (bf16[56,3328]{1,0:T(8,128)(2,1)S(1)}, bf16[56,3328]{1,0:T(8,128)(2,1)S(1)}, u32[]{:S(2)}, u32[]{:S(2)}) collective-permute-start(bf16[56,3328]{1,0:T(8,128)(2,1)S(1)} %fusion.72), channel_id=1, source_target_pairs={{0,8},{4,12},{8,0},{12,4},{16,24},{20,28},{24,16},{28,20},{1,9},{5... | collective-permute-start | bytes 1118216 | tf_op jit(solution)/shard_map/ppermute | solution.py:16
  163.9 41.2 %collective-permute-start.23 = (bf16[224,3328]{1,0:T(8,128)(2,1)S(1)}, bf16[224,3328]{1,0:T(8,128)(2,1)}, u32[]{:S(2)}, u32[]{:S(2)}) collective-permute-start(bf16[224,3328]{1,0:T(8,128)(2,1)S(1)} %bitcast.204), channel_id=1, source_target_pairs={{0,4},{4,0},{8,12},{12,8},{16,20},{20,16},{24,28},{28,24},{1,5},{5... | collective-permute-start | bytes 4472840 | tf_op jit(solution)/shard_map/ppermute | solution.py:16
  166.7 42.0 %collective-permute-start.14 = (bf16[224,3328]{1,0:T(8,128)(2,1)}, bf16[224,3328]{1,0:T(8,128)(2,1)}, u32[]{:S(2)}, u32[]{:S(2)}) collective-permute-start(bf16[224,3328]{1,0:T(8,128)(2,1)} %bitcast.25), channel_id=1, source_target_pairs={{0,4},{4,0},{8,12},{12,8},{16,20},{20,16},{24,28},{28,24},{1,5},{5... | collective-permute-start | bytes 4472840 | tf_op jit(solution)/shard_map/ppermute | solution.py:16
  185.3 19.6 %collective-permute-start.34 = (bf16[2,56,3328]{2,1,0:T(8,128)(2,1)S(1)}, bf16[2,56,3328]{2,1,0:T(8,128)(2,1)S(1)}, u32[]{:S(2)}, u32[]{:S(2)}) collective-permute-start(bf16[2,56,3328]{2,1,0:T(8,128)(2,1)S(1)} %fusion.49), channel_id=1, source_target_pairs={{0,8},{4,12},{8,0},{12,4},{16,24},{20,28},{24,16},{28,20},{1,9},{5... | collective-permute-start | bytes 2236424 | tf_op jit(solution)/shard_map/ppermute | solution.py:16
  196.7 38.5 %collective-permute-start.29 = (bf16[56,3328]{1,0:T(8,128)(2,1)}, bf16[56,3328]{1,0:T(8,128)(2,1)}, u32[]{:S(2)}, u32[]{:S(2)}) collective-permute-start(bf16[56,3328]{1,0:T(8,128)(2,1)} %fusion.76), channel_id=1, source_target_pairs={{0,8},{4,12},{8,0},{12,4},{16,24},{20,28},{24,16},{28,20},{1,9},{5... | collective-permute-start | bytes 1118216 | tf_op jit(solution)/shard_map/ppermute | solution.py:16
  218.6 20.3 %collective-permute-start.35 = (bf16[56,3328]{1,0:T(8,128)(2,1)}, bf16[56,3328]{1,0:T(8,128)(2,1)}, u32[]{:S(2)}, u32[]{:S(2)}) collective-permute-start(bf16[56,3328]{1,0:T(8,128)(2,1)} %fusion.77), channel_id=1, source_target_pairs={{0,16},{4,20},{8,24},{12,28},{16,0},{20,4},{24,8},{28,12},{1,17},{... | collective-permute-start | bytes 1118216 | tf_op jit(solution)/shard_map/ppermute | solution.py:16
  227.9 38.6 %collective-permute-start.24 = (bf16[112,1024]{1,0:T(8,128)(2,1)}, bf16[112,1024]{1,0:T(8,128)(2,1)}, u32[]{:S(2)}, u32[]{:S(2)}) collective-permute-start(bf16[112,1024]{1,0:T(8,128)(2,1)} %get-tuple-element.12), channel_id=1, source_target_pairs={{0,1},{1,2},{2,3},{3,0},{4,5},{5,6},{6,7},{7,4},{8,9},{9,10},{10,1... | collective-permute-start | bytes 688136 | tf_op jit(solution)/shard_map/ppermute | solution.py:31
  231.7 34.7 %collective-permute-start.26 = (bf16[112,1024]{1,0:T(8,128)(2,1)}, bf16[112,1024]{1,0:T(8,128)(2,1)}, u32[]{:S(2)}, u32[]{:S(2)}) collective-permute-start(bf16[112,1024]{1,0:T(8,128)(2,1)} %get-tuple-element.13), channel_id=1, source_target_pairs={{0,3},{1,0},{2,1},{3,2},{4,7},{5,4},{6,5},{7,6},{8,11},{9,8},{10,9... | collective-permute-start | bytes 688136 | tf_op jit(solution)/shard_map/ppermute | solution.py:31
  231.7 34.7 %collective-permute-start.25 = (bf16[112,1024]{1,0:T(8,128)(2,1)}, bf16[112,1024]{1,0:T(8,128)(2,1)}, u32[]{:S(2)}, u32[]{:S(2)}) collective-permute-start(bf16[112,1024]{1,0:T(8,128)(2,1)} %get-tuple-element.14), channel_id=1, source_target_pairs={{0,2},{1,3},{2,0},{3,1},{4,6},{5,7},{6,4},{7,5},{8,10},{9,11},{10,... | collective-permute-start | bytes 688136 | tf_op jit(solution)/shard_map/ppermute | solution.py:31
  246.1 22.5 %collective-permute-start.31 = (bf16[2,56,3328]{2,1,0:T(8,128)(2,1)}, bf16[2,56,3328]{2,1,0:T(8,128)(2,1)}, u32[]{:S(2)}, u32[]{:S(2)}) collective-permute-start(bf16[2,56,3328]{2,1,0:T(8,128)(2,1)} %get-tuple-element.26), channel_id=1, source_target_pairs={{0,16},{4,20},{8,24},{12,28},{16,0},{20,4},{24,8},{28,12},{1,17},{... | collective-permute-start | bytes 2236424 | tf_op jit(solution)/shard_map/ppermute | solution.py:16
  270.6 20.2 %collective-permute-start.32 = (bf16[224,3328]{1,0:T(8,128)(2,1)S(1)}, bf16[224,3328]{1,0:T(8,128)(2,1)S(1)}, u32[]{:S(2)}, u32[]{:S(2)}) collective-permute-start(bf16[224,3328]{1,0:T(8,128)(2,1)S(1)} %bitcast.207), channel_id=1, source_target_pairs={{0,4},{4,0},{8,12},{12,8},{16,20},{20,16},{24,28},{28,24},{1,5},{5... | collective-permute-start | bytes 4472840 | tf_op jit(solution)/shard_map/ppermute | solution.py:16
  307.7 21.2 %collective-permute-start.41 = (bf16[224,3328]{1,0:T(8,128)(2,1)S(1)}, bf16[224,3328]{1,0:T(8,128)(2,1)}, u32[]{:S(2)}, u32[]{:S(2)}) collective-permute-start(bf16[224,3328]{1,0:T(8,128)(2,1)S(1)} %bitcast.212), channel_id=1, source_target_pairs={{0,4},{4,0},{8,12},{12,8},{16,20},{20,16},{24,28},{28,24},{1,5},{5... | collective-permute-start | bytes 4472840 | tf_op jit(solution)/shard_map/ppermute | solution.py:16
  (70 other events, 912.0 us)
where the time goes:
time: 379 us; the launch traced here: 375 us
  matrix products  137 us (36%)
  waiting for transfers between devices  107 us (28%)
  starting transfers between devices  46.7 us (12%)
  other arithmetic  41 us (11%)
  local copies, waits for them, and re-layouts  31.5 us (8%)
  between operations  12.4 us (3%)
    dot_general x15, matrix products, contract(): lax.dot_general(left, right, (((left_dim,), (right_dim,)), ((), ())), pre...  107 us
    ppermute x36, waiting for transfers between devices, swap(): return lax.ppermute(value, 'row', [(i, i ^ bit) for i in range(size)])  79.2 us
    ppermute x36, starting transfers between devices, swap(): return lax.ppermute(value, 'row', [(i, i ^ bit) for i in range(size)])  25.3 us
    ppermute x6, waiting for transfers between devices, gather_col(): lax.ppermute(block, 'col', [(i, (i + shift) % size) for i in range(size)])  23 us
    add x9, other arithmetic, after(): value = value + (first.astype(F32) * 0.0).astype(value.dtype)  16.1 us
    slice x16, local copies, waits for them, and re-layouts, after(): first = lax.slice(other, (0,) * other.ndim, (1,) * other.ndim).reshape(())  15 us
    dot_general x1, matrix products, body(): jnp.dot(after(tokens_t, token_share), up_deltas, preferred_element_type=F32)  13.2 us
    another operation x10, other arithmetic, gather(): total = jnp.stack([total, got], axis=live.index(bit))  12 us
  transfers between devices with their start and end apart: 48, of which 21 were waited for; matrix products, arithmetic and copies ran while one was open for 47% of the time, Pallas kernels for 0%

commit v1 on v0

--- a/solution.py
+++ b/solution.py
@@ -129,6 +129,8 @@
         hid_got = cores(hid_send)
         up_keep = shares(after(tok_keep, hid_send[1]), up_weight, False)
         up = sums(up_keep, up_got)
+        hid_keep = shares(after(cot_keep, up_keep[1]), down_weight, True)
+        hid = sums(hid_keep, hid_got)
         hidden, gate_delta, up_delta = [], [], []
         activated, slope = [], []
         for i in range(2):
@@ -136,8 +138,6 @@
             activated.append(gate[i] * sigmoid_gate)
             hidden.append((activated[i] * up[i]).astype(BF16))
             slope.append(up[i] * sigmoid_gate * (1.0 + gate[i] * (1.0 - sigmoid_gate)))
-        hid_keep = shares(after(cot_keep, *hidden), down_weight, True)
-        hid = sums(hid_keep, hid_got)
         for i in range(2):
             up_delta.append((hid[i] * activated[i]).astype(BF16))
             gate_delta.append((hid[i] * slope[i]).astype(BF16))
@@ -146,11 +146,11 @@
             both = [gather(after(b, *links_free), i, before_core) for i, b in enumerate(blocks)]
             return jnp.concatenate([after(x, *earlier) for x, _ in both], 1), [t for _, t in both]
 
-        hiddens, _ = join(hidden, [], [], *hid_keep)
+        hiddens, _ = join(hidden, [], [], *gate_delta)
         tokens_t = lax.optimization_barrier(tok_all.T)
         out_share = jnp.dot(hiddens, down_weight, preferred_element_type=F32)
         down_grad = contract(hiddens, after(cot_all, out_share), 0, 0).astype(BF16)
-        gate_deltas, gate_mid = join(gate_delta, [], [], down_grad)
+        gate_deltas, gate_mid = join(gate_delta, [], [down_grad])
         gate_grad = jnp.dot(tokens_t, gate_deltas, preferred_element_type=F32).astype(BF16)
         token_share = contract(after(gate_deltas, gate_grad), gate_weight, 1, 1)
         up_deltas, _ = join(up_delta, gate_mid, [gate_grad], token_share)

time: 379 us -> 406 us (1.071)
  waiting for transfers between devices: 107 us -> 123 us
  starting transfers between devices: 46.7 us -> 57.4 us
  other arithmetic: 41 us -> 35.2 us
  local copies, waits for them, and re-layouts: 31.5 us -> 36 us
    ppermute x6, waiting for transfers between devices: 4.42 us -> 13.9 us  [scatter_col(): lax.ppermute(part(me + s).astype(BF16), 'col', [(i, (i + s) % size) for i...]
    ppermute x6, starting transfers between devices: 11.2 us -> 18 us  [scatter_col(): lax.ppermute(part(me + s).astype(BF16), 'col', [(i, (i + s) % size) for i...]
    dot_general x15, matrix products: 107 us -> 102 us  [contract(): lax.dot_general(left, right, (((left_dim,), (right_dim,)), ((), ())), pre...]
    ppermute x36, waiting for transfers between devices: 79.2 us -> 83.5 us  [swap(): return lax.ppermute(value, 'row', [(i, i ^ bit) for i in range(size)])]
    another operation x10 -> x8, other arithmetic: 12 us -> 8.84 us  [gather(): total = jnp.stack([total, got], axis=live.index(bit))]
    slice x16 -> x15, local copies, waits for them, and re-layouts: 15 us -> 13.3 us  [after(): first = lax.slice(other, (0,) * other.ndim, (1,) * other.ndim).reshape(())]
  transfers between devices with their start and end apart: 48 -> 48, of which waited for: 21 -> 21; matrix products, arithmetic and copies ran while one was open for 47% -> 42% of each run, Pallas kernels for 0% -> 0%
where the time goes in v1:
time: 406 us; the launch traced here: 399 us
  matrix products  135 us (33%)
  waiting for transfers between devices  123 us (30%)
  starting transfers between devices  57.4 us (14%)
  local copies, waits for them, and re-layouts  36 us (9%)
  other arithmetic  35.2 us (9%)
  between operations  11.7 us (3%)
    dot_general x15, matrix products, contract(): lax.dot_general(left, right, (((left_dim,), (right_dim,)), ((), ())), pre...  102 us
    ppermute x36, waiting for transfers between devices, swap(): return lax.ppermute(value, 'row', [(i, i ^ bit) for i in range(size)])  83.5 us
    ppermute x36, starting transfers between devices, swap(): return lax.ppermute(value, 'row', [(i, i ^ bit) for i in range(size)])  28.6 us
    ppermute x6, waiting for transfers between devices, gather_col(): lax.ppermute(block, 'col', [(i, (i + shift) % size) for i in range(size)])  26 us
    ppermute x6, starting transfers between devices, scatter_col(): lax.ppermute(part(me + s).astype(BF16), 'col', [(i, (i + s) % size) for i...  18 us
    add x9, other arithmetic, after(): value = value + (first.astype(F32) * 0.0).astype(value.dtype)  14.4 us
    ppermute x6, waiting for transfers between devices, scatter_col(): lax.ppermute(part(me + s).astype(BF16), 'col', [(i, (i + s) % size) for i...  13.9 us
    slice x15, local copies, waits for them, and re-layouts, after(): first = lax.slice(other, (0,) * other.ndim, (1,) * other.ndim).reshape(())  13.3 us
  transfers between devices with their start and end apart: 48, of which 21 were waited for; matrix products, arithmetic and copies ran while one was open for 42% of the time, Pallas kernels for 0%

profile of v1, /device:TPU:0, one launch (start us, length us, event | category | flops | bytes accessed | tf_op | source)
XLA Modules:
  0.0 398.6 jit_solution(13744378666056252768)
XLA Ops:
  12.4 13.8 %collective-permute-done.1 = bf16[112,1024]{1,0:T(8,128)(2,1)S(1)} collective-permute-done((bf16[112,1024]{1,0:T(8,128)(2,1)}, bf16[112,1024]{1,0:T(8,128)(2,1)S(1)}, u32[]{:S(2)}, u32[]{:S(2)}) %collective-permute-start.1) | collective-permute-done | bytes 229408 | tf_op jit(solution)/shard_map/ppermute | solution.py:46
  27.1 6.6 %fusion.12 = f32[224,3328]{1,0:T(8,128)} fusion(bf16[224,1024]{1,0:T(8,128)(2,1)S(1)} %bitcast.237, bf16[1024,6656]{1,0:T(8,128)(2,1)} %param.6), kind=kOutput, calls=%fused_computation.19 | convolution fusion | flops 1526726656 | bytes 10256384 | tf_op jit(solution)/shard_map/dot_general | solution.py:10
  33.7 6.4 %fusion.22 = f32[224,3328]{1,0:T(8,128)} fusion(bf16[224,1024]{1,0:T(8,128)(2,1)S(1)} %bitcast.238, bf16[1024,6656]{1,0:T(8,128)(2,1)} %param.6), kind=kOutput, calls=%fused_computation.29 | convolution fusion | flops 1526726656 | bytes 10256384 | tf_op jit(solution)/shard_map/dot_general | solution.py:10
  59.3 5.4 %collective-permute-done.8 = bf16[112,1024]{1,0:T(8,128)(2,1)S(1)} collective-permute-done((bf16[112,1024]{1,0:T(8,128)(2,1)S(1)}, bf16[112,1024]{1,0:T(8,128)(2,1)S(1)}, u32[]{:S(2)}, u32[]{:S(2)}) %collective-permute-start.8) | collective-permute-done | bytes 229408 | tf_op jit(solution)/shard_map/ppermute | solution.py:46
  65.4 5.7 %fusion.26 = f32[224,3328]{1,0:T(8,128)S(1)} fusion(f32[224,3328]{1,0:T(8,128)} %collective-permute-done.3, bf16[1024,6656]{1,0:T(8,128)(2,1)} %param.6, bf16[224,1024]{1,0:T(8,128)(2,1)S(1)} %bitcast.204, bf16[]{:T(256)} %bitcast.6), kind=kOutput, calls=%fused_computation.36 | convolution fusion | flops 1527701504 | bytes 13238784 | tf_op jit(solution)/shard_map/dot_general | solution.py:10
  71.2 7.3 %fusion.110 = (f32[224,3328]{1,0:T(8,128)S(1)}, f32[224,3328]{1,0:T(8,128)S(1)}) fusion(f32[224,3328]{1,0:T(8,128)} %collective-permute-done.24, bf16[1024,6656]{1,0:T(8,128)(2,1)} %param.6, bf16[224,1024]{1,0:T(8,128)(2,1)S(1)} %bitcast.205, bf16[]{:T(256)} %bitcast.6), kind=kOutput, calls=%fused_computation.183 | convolution fusion | flops 1527701504 | bytes 16220672 | tf_op jit(solution)/shard_map/dot_general | solution.py:10
  85.5 5.5 %fusion.32 = f32[224,3328]{1,0:T(8,128)S(1)} fusion(f32[224,3328]{1,0:T(8,128)} %collective-permute-done.9, bf16[1024,6656]{1,0:T(8,128)(2,1)} %param.7, bf16[224,1024]{1,0:T(8,128)(2,1)S(1)} %bitcast.206, bf16[]{:T(256)} %bitcast.16), kind=kOutput, calls=%fused_computation.38 | convolution fusion | flops 1527701504 | bytes 13238784 | tf_op jit(solution)/shard_map/dot_general | solution.py:10
  93.6 5.5 %fusion.109 = (f32[224,3328]{1,0:T(8,128)S(1)}, f32[224,3328]{1,0:T(8,128)S(1)}) fusion(f32[224,3328]{1,0:T(8,128)} %collective-permute-done.21, bf16[1024,6656]{1,0:T(8,128)(2,1)} %param.7, bf16[224,1024]{1,0:T(8,128)(2,1)S(1)} %bitcast.207, bf16[]{:T(256)} %bitcast.16), kind=kOutput, calls=%fused_computation.182 | convolution fusion | flops 1527701504 | bytes 16220672 | tf_op jit(solution)/shard_map/dot_general | solution.py:10
  112.5 6.4 %collective-permute-done.25 = bf16[2,56,3328]{2,1,0:T(8,128)(2,1)S(1)} collective-permute-done((bf16[2,56,3328]{2,1,0:T(8,128)(2,1)S(1)}, bf16[2,56,3328]{2,1,0:T(8,128)(2,1)S(1)}, u32[]{:S(2)}, u32[]{:S(2)}) %collective-permute-start.25) | collective-permute-done | bytes 745504 | tf_op jit(solution)/shard_map/ppermute | solution.py:16
  121.3 5.8 %collective-permute-done.10 = bf16[2,56,3328]{2,1,0:T(8,128)(2,1)S(1)} collective-permute-done((bf16[2,56,3328]{2,1,0:T(8,128)(2,1)}, bf16[2,56,3328]{2,1,0:T(8,128)(2,1)S(1)}, u32[]{:S(2)}, u32[]{:S(2)}) %collective-permute-start.10) | collective-permute-done | bytes 745504 | tf_op jit(solution)/shard_map/ppermute | solution.py:16
  129.6 5.2 %collective-permute-done.22 = bf16[2,56,3328]{2,1,0:T(8,128)(2,1)S(1)} collective-permute-done((bf16[2,56,3328]{2,1,0:T(8,128)(2,1)S(1)}, bf16[2,56,3328]{2,1,0:T(8,128)(2,1)S(1)}, u32[]{:S(2)}, u32[]{:S(2)}) %collective-permute-start.22) | collective-permute-done | bytes 745504 | tf_op jit(solution)/shard_map/ppermute | solution.py:16
  148.4 14.0 %collective-permute-done.16 = bf16[2,56,3328]{2,1,0:T(8,128)(2,1)S(1)} collective-permute-done((bf16[2,56,3328]{2,1,0:T(8,128)(2,1)S(1)}, bf16[2,56,3328]{2,1,0:T(8,128)(2,1)S(1)}, u32[]{:S(2)}, u32[]{:S(2)}) %collective-permute-start.16) | collective-permute-done | bytes 745504 | tf_op jit(solution)/shard_map/ppermute | solution.py:16
  163.3 16.1 %collective-permute-done.19 = bf16[2,56,3328]{2,1,0:T(8,128)(2,1)S(1)} collective-permute-done((bf16[2,56,3328]{2,1,0:T(8,128)(2,1)S(1)}, bf16[2,56,3328]{2,1,0:T(8,128)(2,1)S(1)}, u32[]{:S(2)}, u32[]{:S(2)}) %collective-permute-start.19) | collective-permute-done | bytes 745504 | tf_op jit(solution)/shard_map/ppermute | solution.py:16
  182.1 5.4 %collective-permute-done.17 = bf16[56,3328]{1,0:T(8,128)(2,1)S(1)} collective-permute-done((bf16[56,3328]{1,0:T(8,128)(2,1)S(1)}, bf16[56,3328]{1,0:T(8,128)(2,1)S(1)}, u32[]{:S(2)}, u32[]{:S(2)}) %collective-permute-start.17) | collective-permute-done | bytes 372768 | tf_op jit(solution)/shard_map/ppermute | solution.py:16
  207.6 9.1 %collective-permute-done.13 = bf16[2,56,3328]{2,1,0:T(8,128)(2,1)} collective-permute-done((bf16[2,56,3328]{2,1,0:T(8,128)(2,1)}, bf16[2,56,3328]{2,1,0:T(8,128)(2,1)}, u32[]{:S(2)}, u32[]{:S(2)}) %collective-permute-start.13) | collective-permute-done | bytes 745504 | tf_op jit(solution)/shard_map/ppermute | solution.py:16
  229.0 6.9 %collective-permute-done.36 = bf16[56,3328]{1,0:T(8,128)(2,1)S(1)} collective-permute-done((bf16[56,3328]{1,0:T(8,128)(2,1)S(1)}, bf16[56,3328]{1,0:T(8,128)(2,1)S(1)}, u32[]{:S(2)}, u32[]{:S(2)}) %collective-permute-start.36) | collective-permute-done | bytes 372768 | tf_op jit(solution)/shard_map/ppermute | solution.py:16
  241.2 6.5 %fusion.39 = f32[448,1024]{1,0:T(8,128)S(1)} fusion(bf16[6656,1024]{1,0:T(8,128)(2,1)S(1)} %bitcast.195, bf16[448,3328]{1,0:T(8,128)(2,1)S(1)} %fusion.41, bf16[448,3328]{1,0:T(8,128)(2,1)S(1)} %fusion.40), kind=kOutput, calls=%fused_computation.41 | convolution fusion | flops 6118834176 | bytes 21430272 | tf_op jit(solution)/shard_map/dot_general | solution.py:151
  249.6 13.4 %convolution_convert_fusion.2 = bf16[6656,1024]{1,0:T(8,128)(2,1)} fusion(bf16[448,3328]{1,0:T(8,128)(2,1)} %copy-done.8, bf16[448,3328]{1,0:T(8,128)(2,1)} %copy-done.7, bf16[224,1024]{1,0:T(8,128)(2,1)S(1)} %bitcast.252, bf16[224,1024]{1,0:T(8,128)(2,1)S(1)} %bitcast.226, bf16[]{:T(256)} %bitcast.65), kind=kOutput, calls=%fused_computation.6 | convolution fusion | flops 6128402432 | bytes 20512770 | tf_op jit(solution)/shard_map/dot_general | solution.py:10
  278.7 5.6 %collective-permute-start.30 = (bf16[112,1024]{1,0:T(8,128)(2,1)S(1)}, bf16[112,1024]{1,0:T(8,128)(2,1)S(1)}, u32[]{:S(2)}, u32[]{:S(2)}) collective-permute-start(bf16[112,1024]{1,0:T(8,128)(2,1)S(1)} %get-tuple-element.16), channel_id=1, source_target_pairs={{0,1},{1,2},{2,3},{3,0},{4,5},{5,6},{6,7},{7,4},{8,9},{9,10},{10,1... | collective-permute-start | bytes 688136 | tf_op jit(solution)/shard_map/ppermute | solution.py:31
  296.6 8.6 %collective-permute-done.31 = bf16[112,1024]{1,0:T(8,128)(2,1)S(1)} collective-permute-done((bf16[112,1024]{1,0:T(8,128)(2,1)S(1)}, bf16[112,1024]{1,0:T(8,128)(2,1)S(1)}, u32[]{:S(2)}, u32[]{:S(2)}) %collective-permute-start.31) | collective-permute-done | bytes 229408 | tf_op jit(solution)/shard_map/ppermute | solution.py:31
  311.2 13.2 %convolution_convert_fusion.1 = bf16[1024,6656]{1,0:T(8,128)(2,1)} fusion(bf16[1024,448]{0,1:T(8,128)(2,1)S(1)} %copy-done.26, bf16[224,3328]{1,0:T(8,128)(2,1)} %collective-permute-done.38, bf16[224,3328]{1,0:T(8,128)(2,1)} %bitcast.72, bf16[224,3328]{1,0:T(8,128)(2,1)} %collective-permute-done.35, bf16[224,3328]{1,0:T(8,128)(2,1)} %bitcast.67), kind=kOutput, calls=%fused_computation.5 | convolution fusion | flops 6137577472 | bytes 20512768 | tf_op jit(solution)/shard_map/dot_general | solution.py:154
  330.0 14.2 %fusion.24 = f32[448,1024]{1,0:T(8,128)} fusion(bf16[1024,6656]{1,0:T(8,128)(2,1)} %param.6, bf16[]{:T(256)} %bitcast.74, bf16[224,3328]{1,0:T(8,128)(2,1)} %collective-permute-done.38, bf16[224,3328]{1,0:T(8,128)(2,1)} %bitcast.72, bf16[224,3328]{1,0:T(8,128)(2,1)} %collective-permute-done.35, bf16[224,3328]{1,0:T(8,128)(2,1)} %bitcast.67), kind=kOutput, calls=%fused_computation.34 | convolution fusion | flops 6136725504 | bytes 21430274 | tf_op jit(solution)/shard_map/dot_general | solution.py:10
  353.0 14.4 %fusion.43 = f32[448,1024]{1,0:T(8,128)S(1)} fusion(f32[448,1024]{1,0:T(8,128)} %fusion.24, bf16[1024,6656]{1,0:T(8,128)(2,1)} %param.7, bf16[448,3328]{1,0:T(8,128)(2,1)} %maximum_add_fusion.3, bf16[448,3328]{1,0:T(8,128)(2,1)} %maximum_add_fusion.2), kind=kOutput, calls=%fused_computation.51 | convolution fusion | flops 6119292928 | bytes 23265280 | tf_op jit(solution)/shard_map/dot_general | solution.py:10
  381.2 13.1 %convolution_convert_fusion = bf16[1024,6656]{1,0:T(8,128)(2,1)} fusion(bf16[448,3328]{1,0:T(8,128)(2,1)} %maximum_add_fusion.3, bf16[448,3328]{1,0:T(8,128)(2,1)} %maximum_add_fusion.2, bf16[1024,448]{0,1:T(8,128)(2,1)S(1)} %copy-done.27, bf16[]{:T(256)} %bitcast.95), kind=kOutput, calls=%fused_computation.4 | convolution fusion | flops 6126108672 | bytes 20512770 | tf_op jit(solution)/shard_map/dot_general | solution.py:158
  (268 shorter events, 172.8 us)
Async XLA Ops:
  3.7 22.6 %collective-permute-start.2 = (bf16[112,1024]{1,0:T(8,128)(2,1)}, bf16[112,1024]{1,0:T(8,128)(2,1)S(1)}, u32[]{:S(2)}, u32[]{:S(2)}) collective-permute-start(bf16[112,1024]{1,0:T(8,128)(2,1)} %param.5), channel_id=1, source_target_pairs={{0,3},{1,0},{2,1},{3,2},{4,7},{5,4},{6,5},{7,6},{8,11},{9,8},{10,9... | collective-permute-start | bytes 688136 | tf_op jit(solution)/shard_map/ppermute | solution.py:46
  5.8 20.5 %collective-permute-start.1 = (bf16[112,1024]{1,0:T(8,128)(2,1)}, bf16[112,1024]{1,0:T(8,128)(2,1)S(1)}, u32[]{:S(2)}, u32[]{:S(2)}) collective-permute-start(bf16[112,1024]{1,0:T(8,128)(2,1)} %param.5), channel_id=1, source_target_pairs={{0,2},{1,3},{2,0},{3,1},{4,6},{5,7},{6,4},{7,5},{8,10},{9,11},{10,... | collective-permute-start | bytes 688136 | tf_op jit(solution)/shard_map/ppermute | solution.py:46
  33.7 31.7 %collective-permute-start.3 = (f32[224,3328]{1,0:T(8,128)}, f32[224,3328]{1,0:T(8,128)}, u32[]{:S(2)}, u32[]{:S(2)}) collective-permute-start(f32[224,3328]{1,0:T(8,128)} %fusion.12), channel_id=1, source_target_pairs={{0,4},{4,0},{8,12},{12,8},{16,20},{20,16},{24,28},{28,24},{1,5},{5... | collective-permute-start | bytes 8945672 | tf_op jit(solution)/shard_map/ppermute | solution.py:16
  40.1 31.1 %collective-permute-start.24 = (f32[224,3328]{1,0:T(8,128)}, f32[224,3328]{1,0:T(8,128)}, u32[]{:S(2)}, u32[]{:S(2)}) collective-permute-start(f32[224,3328]{1,0:T(8,128)} %fusion.22), channel_id=1, source_target_pairs={{0,4},{4,0},{8,12},{12,8},{16,20},{20,16},{24,28},{28,24},{1,5},{5... | collective-permute-start | bytes 8945672 | tf_op jit(solution)/shard_map/ppermute | solution.py:16
  49.3 36.2 %collective-permute-start.9 = (f32[224,3328]{1,0:T(8,128)}, f32[224,3328]{1,0:T(8,128)}, u32[]{:S(2)}, u32[]{:S(2)}) collective-permute-start(f32[224,3328]{1,0:T(8,128)} %fusion.4), channel_id=1, source_target_pairs={{0,4},{4,0},{8,12},{12,8},{16,20},{20,16},{24,28},{28,24},{1,5},{5... | collective-permute-start | bytes 8945672 | tf_op jit(solution)/shard_map/ppermute | solution.py:16
  59.2 34.4 %collective-permute-start.21 = (f32[224,3328]{1,0:T(8,128)}, f32[224,3328]{1,0:T(8,128)}, u32[]{:S(2)}, u32[]{:S(2)}) collective-permute-start(f32[224,3328]{1,0:T(8,128)} %fusion.18), channel_id=1, source_target_pairs={{0,4},{4,0},{8,12},{12,8},{16,20},{20,16},{24,28},{28,24},{1,5},{5... | collective-permute-start | bytes 8945672 | tf_op jit(solution)/shard_map/ppermute | solution.py:16
  92.1 51.5 %collective-permute-start.18 = (f32[224,3328]{1,0:T(8,128)}, f32[224,3328]{1,0:T(8,128)}, u32[]{:S(2)}, u32[]{:S(2)}) collective-permute-start(f32[224,3328]{1,0:T(8,128)} %fusion.10), channel_id=1, source_target_pairs={{0,4},{4,0},{8,12},{12,8},{16,20},{20,16},{24,28},{28,24},{1,5},{5... | collective-permute-start | bytes 8945672 | tf_op jit(solution)/shard_map/ppermute | solution.py:16
  100.8 26.3 %collective-permute-start.10 = (bf16[2,56,3328]{2,1,0:T(8,128)(2,1)}, bf16[2,56,3328]{2,1,0:T(8,128)(2,1)S(1)}, u32[]{:S(2)}, u32[]{:S(2)}) collective-permute-start(bf16[2,56,3328]{2,1,0:T(8,128)(2,1)} %bitcast.18), channel_id=1, source_target_pairs={{0,16},{4,20},{8,24},{12,28},{16,0},{20,4},{24,8},{28,12},{1,17},{... | collective-permute-start | bytes 2236424 | tf_op jit(solution)/shard_map/ppermute | solution.py:16
  102.5 32.3 %collective-permute-start.22 = (bf16[2,56,3328]{2,1,0:T(8,128)(2,1)S(1)}, bf16[2,56,3328]{2,1,0:T(8,128)(2,1)S(1)}, u32[]{:S(2)}, u32[]{:S(2)}) collective-permute-start(bf16[2,56,3328]{2,1,0:T(8,128)(2,1)S(1)} %fusion.51), channel_id=1, source_target_pairs={{0,8},{4,12},{8,0},{12,4},{16,24},{20,28},{24,16},{28,20},{1,9},{5... | collective-permute-start | bytes 2236424 | tf_op jit(solution)/shard_map/ppermute | solution.py:16
  111.5 25.7 %collective-permute-start.15 = (f32[224,3328]{1,0:T(8,128)}, f32[224,3328]{1,0:T(8,128)S(1)}, u32[]{:S(2)}, u32[]{:S(2)}) collective-permute-start(f32[224,3328]{1,0:T(8,128)} %fusion), channel_id=1, source_target_pairs={{0,4},{4,0},{8,12},{12,8},{16,20},{20,16},{24,28},{28,24},{1,5},{5... | collective-permute-start | bytes 8945672 | tf_op jit(solution)/shard_map/ppermute | solution.py:16
  118.9 61.3 %collective-permute-start.5 = (bf16[56,3328]{1,0:T(8,128)(2,1)}, bf16[56,3328]{1,0:T(8,128)(2,1)S(1)}, u32[]{:S(2)}, u32[]{:S(2)}) collective-permute-start(bf16[56,3328]{1,0:T(8,128)(2,1)} %fusion.77), channel_id=1, source_target_pairs={{0,8},{4,12},{8,0},{12,4},{16,24},{20,28},{24,16},{28,20},{1,9},{5... | collective-permute-start | bytes 1118216 | tf_op jit(solution)/shard_map/ppermute | solution.py:16
  127.1 63.2 %collective-permute-start.26 = (bf16[56,3328]{1,0:T(8,128)(2,1)}, bf16[56,3328]{1,0:T(8,128)(2,1)S(1)}, u32[]{:S(2)}, u32[]{:S(2)}) collective-permute-start(bf16[56,3328]{1,0:T(8,128)(2,1)} %fusion.82), channel_id=1, source_target_pairs={{0,16},{4,20},{8,24},{12,28},{16,0},{20,4},{24,8},{28,12},{1,17},{... | collective-permute-start | bytes 1118216 | tf_op jit(solution)/shard_map/ppermute | solution.py:16
  134.8 47.3 %collective-permute-start.11 = (bf16[56,3328]{1,0:T(8,128)(2,1)}, bf16[56,3328]{1,0:T(8,128)(2,1)}, u32[]{:S(2)}, u32[]{:S(2)}) collective-permute-start(bf16[56,3328]{1,0:T(8,128)(2,1)} %fusion.78), channel_id=1, source_target_pairs={{0,8},{4,12},{8,0},{12,4},{16,24},{20,28},{24,16},{28,20},{1,9},{5... | collective-permute-start | bytes 1118216 | tf_op jit(solution)/shard_map/ppermute | solution.py:16
  137.2 53.1 %collective-permute-start.23 = (bf16[56,3328]{1,0:T(8,128)(2,1)}, bf16[56,3328]{1,0:T(8,128)(2,1)}, u32[]{:S(2)}, u32[]{:S(2)}) collective-permute-start(bf16[56,3328]{1,0:T(8,128)(2,1)} %fusion.81), channel_id=1, source_target_pairs={{0,16},{4,20},{8,24},{12,28},{16,0},{20,4},{24,8},{28,12},{1,17},{... | collective-permute-start | bytes 1118216 | tf_op jit(solution)/shard_map/ppermute | solution.py:16
  207.2 20.2 %collective-permute-start.33 = (bf16[56,3328]{1,0:T(8,128)(2,1)}, bf16[56,3328]{1,0:T(8,128)(2,1)S(1)}, u32[]{:S(2)}, u32[]{:S(2)}) collective-permute-start(bf16[56,3328]{1,0:T(8,128)(2,1)} %get-tuple-element.8), channel_id=1, source_target_pairs={{0,8},{4,12},{8,0},{12,4},{16,24},{20,28},{24,16},{28,20},{1,9},{5... | collective-permute-start | bytes 1118216 | tf_op jit(solution)/shard_map/ppermute | solution.py:16
  218.2 19.8 %collective-permute-start.14 = (bf16[224,3328]{1,0:T(8,128)(2,1)S(1)}, bf16[224,3328]{1,0:T(8,128)(2,1)S(1)}, u32[]{:S(2)}, u32[]{:S(2)}) collective-permute-start(bf16[224,3328]{1,0:T(8,128)(2,1)S(1)} %bitcast.212), channel_id=1, source_target_pairs={{0,4},{4,0},{8,12},{12,8},{16,20},{20,16},{24,28},{28,24},{1,5},{5... | collective-permute-start | bytes 4472840 | tf_op jit(solution)/shard_map/ppermute | solution.py:16
  228.7 36.5 %collective-permute-start.34 = (bf16[2,56,3328]{2,1,0:T(8,128)(2,1)}, bf16[2,56,3328]{2,1,0:T(8,128)(2,1)}, u32[]{:S(2)}, u32[]{:S(2)}) collective-permute-start(bf16[2,56,3328]{2,1,0:T(8,128)(2,1)} %get-tuple-element.30), channel_id=1, source_target_pairs={{0,16},{4,20},{8,24},{12,28},{16,0},{20,4},{24,8},{28,12},{1,17},{... | collective-permute-start | bytes 2236424 | tf_op jit(solution)/shard_map/ppermute | solution.py:16
  237.1 28.1 %collective-permute-start.37 = (bf16[2,56,3328]{2,1,0:T(8,128)(2,1)}, bf16[2,56,3328]{2,1,0:T(8,128)(2,1)}, u32[]{:S(2)}, u32[]{:S(2)}) collective-permute-start(bf16[2,56,3328]{2,1,0:T(8,128)(2,1)} %get-tuple-element.32), channel_id=1, source_target_pairs={{0,8},{4,12},{8,0},{12,4},{16,24},{20,28},{24,16},{28,20},{1,9},{5... | collective-permute-start | bytes 2236424 | tf_op jit(solution)/shard_map/ppermute | solution.py:16
  269.3 41.9 %collective-permute-start.38 = (bf16[224,3328]{1,0:T(8,128)(2,1)}, bf16[224,3328]{1,0:T(8,128)(2,1)}, u32[]{:S(2)}, u32[]{:S(2)}) collective-permute-start(bf16[224,3328]{1,0:T(8,128)(2,1)} %bitcast.72), channel_id=1, source_target_pairs={{0,4},{4,0},{8,12},{12,8},{16,20},{20,16},{24,28},{28,24},{1,5},{5... | collective-permute-start | bytes 4472840 | tf_op jit(solution)/shard_map/ppermute | solution.py:16
  271.7 39.5 %collective-permute-start.35 = (bf16[224,3328]{1,0:T(8,128)(2,1)}, bf16[224,3328]{1,0:T(8,128)(2,1)}, u32[]{:S(2)}, u32[]{:S(2)}) collective-permute-start(bf16[224,3328]{1,0:T(8,128)(2,1)} %bitcast.67), channel_id=1, source_target_pairs={{0,4},{4,0},{8,12},{12,8},{16,20},{20,16},{24,28},{28,24},{1,5},{5... | collective-permute-start | bytes 4472840 | tf_op jit(solution)/shard_map/ppermute | solution.py:16
  284.8 20.5 %collective-permute-start.31 = (bf16[112,1024]{1,0:T(8,128)(2,1)S(1)}, bf16[112,1024]{1,0:T(8,128)(2,1)S(1)}, u32[]{:S(2)}, u32[]{:S(2)}) collective-permute-start(bf16[112,1024]{1,0:T(8,128)(2,1)S(1)} %get-tuple-element.18), channel_id=1, source_target_pairs={{0,2},{1,3},{2,0},{3,1},{4,6},{5,7},{6,4},{7,5},{8,10},{9,11},{10,... | collective-permute-start | bytes 688136 | tf_op jit(solution)/shard_map/ppermute | solution.py:31
  329.5 20.1 %collective-permute-start.41 = (bf16[224,3328]{1,0:T(8,128)(2,1)S(1)}, bf16[224,3328]{1,0:T(8,128)(2,1)}, u32[]{:S(2)}, u32[]{:S(2)}) collective-permute-start(bf16[224,3328]{1,0:T(8,128)(2,1)S(1)} %bitcast.216), channel_id=1, source_target_pairs={{0,4},{4,0},{8,12},{12,8},{16,20},{20,16},{24,28},{28,24},{1,5},{5... | collective-permute-start | bytes 4472840 | tf_op jit(solution)/shard_map/ppermute | solution.py:16
  372.3 22.1 %collective-permute-start.45 = (bf16[112,1024]{1,0:T(8,128)(2,1)S(1)}, bf16[112,1024]{1,0:T(8,128)(2,1)S(1)}, u32[]{:S(2)}, u32[]{:S(2)}) collective-permute-start(bf16[112,1024]{1,0:T(8,128)(2,1)S(1)} %get-tuple-element.11), channel_id=1, source_target_pairs={{0,1},{1,2},{2,3},{3,0},{4,5},{5,6},{6,7},{7,4},{8,9},{9,10},{10,1... | collective-permute-start | bytes 688136 | tf_op jit(solution)/shard_map/ppermute | solution.py:31
  376.1 20.4 %collective-permute-start.46 = (bf16[112,1024]{1,0:T(8,128)(2,1)S(1)}, bf16[112,1024]{1,0:T(8,128)(2,1)S(1)}, u32[]{:S(2)}, u32[]{:S(2)}) collective-permute-start(bf16[112,1024]{1,0:T(8,128)(2,1)S(1)} %get-tuple-element.13), channel_id=1, source_target_pairs={{0,2},{1,3},{2,0},{3,1},{4,6},{5,7},{6,4},{7,5},{8,10},{9,11},{10,... | collective-permute-start | bytes 688136 | tf_op jit(solution)/shard_map/ppermute | solution.py:31
  (69 other events, 997.5 us)
